TPU v7x, 32 devices: a whole 2x2x4 slice. The times are simulated.
32 devices in a mesh: groups: 2 (over x), rows: 16 (over z, y, core).
Axes of the slice: x: 2, y: 2, z: 4, core: 2. Of those that a mesh axis runs over, the one named last changes fastest.
Arguments:
- a_blocks: bfloat16 [256, 8, 256, 256], P(('groups', 'rows')), parts along dimension 0, may hold values from -8 to 8
- basis_in: bfloat16 [65536, 128], P(('groups', 'rows')), parts along dimension 0, may hold values from -5 to 5
- pattern: int32 [256, 8], P(('groups', 'rows')), parts along dimension 0, may hold values from 0 to 127, as said below
Outputs:
- basis_out: float32 [65536, 128], P(('groups', 'rows')), parts along dimension 0
- factor: float32 [256, 128], P('groups'), parts along dimension 0
There are 2 independent parts, one for each index of `groups`. A program takes and returns all parts, laid end to end along the dimension named above; each array names one. Nothing has to cross between parts.
Inputs may be any that keep to these rules, and one draw needn't show every extreme that they name: `pattern`: the 64 entries of the block rows of one device name blocks of at most 15 other devices; those naming blocks of any one other device number at most 5 and name at most 1 distinct blocks; all three bounds are reached in every draw. The entries of one block row that name blocks of other devices are distinct.
All inputs are finite; a program needn't handle non-finite values.
Results may differ from a plain program's by a relative error of at most 0.0003.
Values may be sent and summed in bfloat16 or wider, within the bound.
A program may use at most 128 MiB of HBM per device.

v0:
```python
import jax
import jax.numpy as jnp
from jax import lax
from jax.sharding import PartitionSpec as P


def upper_factor_of(matrix):
    return jnp.linalg.cholesky(matrix).T


def shards(a_blocks, basis_in, pattern):
    rank_count = lax.axis_size("rows")
    my_index = lax.axis_index("rows")
    block_rows, slot_count, block_size, unused = a_blocks.shape
    columns = basis_in.shape[1]
    own_blocks = basis_in.reshape(block_rows, block_size, columns)
    ref_count = block_rows * slot_count
    my_cols = pattern.reshape(ref_count)
    my_owner = my_cols // block_rows
    my_local = my_cols - my_owner * block_rows
    remote = my_owner != my_index
    every = lax.all_gather(pattern, "rows", axis=0, tiled=True).reshape(rank_count, ref_count)
    their_owner = every // block_rows
    their_local = every - their_owner * block_rows
    readers = jnp.arange(rank_count, dtype=jnp.int32)
    block_ids = jnp.arange(block_rows, dtype=jnp.int32)
    wanted = (their_owner == my_index) & (readers[:, None] != my_index)
    owners_hot = (my_owner[:, None] == readers[None, :]) & remote[:, None]
    owner_slots = min(ref_count - 1, rank_count - 1)
    slot_depth = (ref_count + owner_slots - 1) // owner_slots
    wanted_int = wanted.astype(jnp.int32)
    rank_in = jnp.cumsum(wanted_int, axis=1) - wanted_int
    by_slot = wanted[:, :, None] & (
        rank_in[:, :, None] == jnp.arange(slot_depth, dtype=jnp.int32)[None, None, :]
    )
    by_block = their_local[:, :, None] == block_ids[None, None, :]
    selection = jnp.einsum(
        "erk,erb->ekb",
        by_slot.astype(jnp.bfloat16),
        by_block.astype(jnp.bfloat16),
        preferred_element_type=jnp.float32,
    ).astype(jnp.bfloat16)
    outgoing = jnp.einsum(
        "ekb,bij->ekij", selection, own_blocks, preferred_element_type=jnp.float32
    ).astype(jnp.bfloat16)
    incoming = lax.all_to_all(outgoing, "rows", split_axis=0, concat_axis=0, tiled=True)
    hot_int = owners_hot.astype(jnp.int32)
    mine_rank = jnp.cumsum(hot_int, axis=0) - hot_int
    slot_index = jnp.sum(mine_rank * hot_int, axis=1)
    far_index = jnp.where(remote, my_owner * slot_depth + slot_index, 0)
    far_part = jnp.take(
        incoming.reshape(rank_count * slot_depth, block_size, columns), far_index, axis=0
    )
    local_part = jnp.take(own_blocks, my_local, axis=0)
    operand = jnp.where(remote[:, None, None], far_part, local_part).reshape(
        block_rows, slot_count, block_size, columns
    )
    product = jnp.einsum("rsij,rsjk->rik", a_blocks, operand, preferred_element_type=jnp.float32)
    image = product.reshape(block_rows * block_size, columns)
    node_count = rank_count * block_rows * block_size
    gram_local = jnp.einsum("nk,nl->kl", image, image, precision=lax.Precision.HIGHEST)
    gram = lax.psum(gram_local, "rows")
    factor = upper_factor_of(gram / node_count)
    basis_out = jax.scipy.linalg.solve_triangular(factor.T, image.T, lower=True).T
    return (basis_out, factor)


def solution(mesh):
    placed = (
        P(("groups", "rows"), None, None, None),
        P(("groups", "rows"), None),
        P(("groups", "rows"), None),
    )
    return jax.shard_map(
        shards,
        mesh=mesh,
        in_specs=placed,
        out_specs=(P(("groups", "rows"), None), P("groups", None)),
        check_vma=False,
    )
```

profile of v0, /device:TPU:8, one launch (start us, length us, event | category | flops | bytes accessed | tf_op | source)
XLA Modules:
  0.0 299.5 jit_solution(1078787044356833225)
XLA Ops:
  7.2 19.3 %all_gather.3 = s32[128,8]{1,0:T(8,128)S(1)} all-gather(s32[8,8]{1,0:T(8,128)} %param.5), channel_id=1, replica_groups=mesh['groups'=2,'rows'=16] {'rows'}, dimensions={0}, use_global_device_ids=true | all-gather | bytes 4352 | tf_op jit(solution)/shard_map/all_gather | solution.py:22
  26.4 0.1 reshape.362
  26.5 0.1 fusion.33
  26.6 0.2 reduce_window_sum.23
  26.8 0.1 fusion.11
  27.0 2.5 convolution_convert_fusion
  29.5 3.7 %copy.22 = bf16[16,5,256,128]{3,2,1,0:T(8,128)(2,1)} copy(bf16[16,5,256,128]{3,0,2,1:T(8,128)(2,1)S(1)} %convolution_convert_fusion) | data formatting | bytes 10485760 | tf_op jit(solution)/shard_map/convert_element_type | solution.py:45
  33.3 7.7 %all-to-all-start = ((bf16[16,5,256,128]{3,2,1,0:T(8,128)(2,1)}), bf16[16,5,256,128]{3,2,1,0:T(8,128)(2,1)}, u32[]{:S(2)}, u32[]{:S(2)}) async-start(bf16[16,5,256,128]{3,2,1,0:T(8,128)(2,1)} %copy.22), calls=%async_computation | async-start | bytes 10485760 | tf_op jit(solution)/shard_map/all_to_all | solution.py:46
  41.0 0.1 reshape.361
  41.1 0.1 reshape.365
  41.2 0.1 fusion.23
  41.3 0.1 reduce_window_sum.22
  41.4 0.2 select_reduce_fusion.1
  41.6 0.1 reduce_sum.14
  41.7 3.1 %gather_fusion.1 = bf16[64,256,128]{2,1,0:T(8,128)(2,1)} fusion(bf16[8,256,128]{2,1,0:T(8,128)(2,1)S(1)} %bitcast.43, s32[1024]{0:T(1024)S(1)} %pad_clamp_fusion), kind=kCustom, calls=%fused_computation.1 | custom fusion | bytes 8388864 | tf_op jit(solution)/shard_map/jit(_take)/gather | solution.py:54
  44.8 6.4 %copy.24 = bf16[64,256,128]{1,2,0:T(8,128)(2,1)} copy(bf16[64,256,128]{2,1,0:T(8,128)(2,1)} %gather_fusion.1) | data formatting | bytes 8388608 | tf_op jit(solution)/shard_map/jit(_take)/gather | solution.py:54
  51.2 103.1 %all-to-all-done = bf16[16,5,256,128]{3,2,1,0:T(8,128)(2,1)} async-done(((bf16[16,5,256,128]{3,2,1,0:T(8,128)(2,1)}), bf16[16,5,256,128]{3,2,1,0:T(8,128)(2,1)}, u32[]{:S(2)}, u32[]{:S(2)}) %all-to-all-start) | async-done | bytes 5242912 | tf_op jit(solution)/shard_map/all_to_all | solution.py:46
  154.3 5.6 %gather_fusion = bf16[64,256,128]{2,1,0:T(8,128)(2,1)} fusion(bf16[80,256,128]{2,1,0:T(8,128)(2,1)} %bitcast.3, s32[1024]{0:T(1024)S(1)} %pad_clamp_fusion.1), kind=kCustom, calls=%fused_computation | custom fusion | bytes 8388864 | tf_op jit(solution)/shard_map/jit(_take)/gather | solution.py:51
  159.8 6.4 %copy.23 = bf16[8,8,256,128]{2,3,1,0:T(8,128)(2,1)} copy(bf16[8,8,256,128]{3,2,1,0:T(8,128)(2,1)} %bitcast.44) | data formatting | bytes 8388608 | tf_op jit(solution)/shard_map/jit(_take)/gather | solution.py:51
  166.3 8.7 %fusion.8 = f32[8,256,128]{1,2,0:T(8,128)S(1)} fusion(bf16[8,8,256,256]{3,2,1,0:T(8,128)(2,1)} %param.3, bf16[8,8,256,128]{2,3,1,0:T(8,128)(2,1)} %bitcast.45, bf16[8,8,256,128]{2,3,1,0:T(8,128)(2,1)} %copy.23, pred[8,8]{1,0:T(8,128)(4,1)S(1)} %get-tuple-element.17, pred[8,8]{1,0:T(8,128)(4,1)S(1)} %get-tuple-element.18, pred[8,8]{1,0:T(8,128)(4,1)S(1)} %get-tuple-element.16), kind=kOutput, calls=%fused_computation.11 | convolution fusion | flops 1080033280 | bytes 17825984 | tf_op jit(solution)/shard_map/rsij,rsjk->rik/dot_general | solution.py:58
  175.0 1.6 convolution_bitcast_fusion
  176.7 0.3 copy.25
  177.0 88.3 %all-reduce.2.cloned.1.call-done = f32[128,128]{0,1:T(8,128)} async-done(((f32[128,128]{0,1:T(8,128)}), f32[128,128]{0,1:T(8,128)}) %all-reduce.2.cloned.1.call-update) | async-done | bytes 65552 | tf_op jit(solution)/shard_map/psum | solution.py:62
  265.3 0.8 broadcast_multiply_fusion
  266.1 0.1 copy.28
  266.2 0.9 fusion.16
  267.1 11.7 %cholesky.16 = f32[128,128]{1,0:T(8,128)S(1)} custom-call(f32[128,128]{1,0:T(8,128)S(1)} %fusion.16), custom_call_target="Cholesky" | custom-call | tf_op jit(solution)/shard_map/jit(cholesky)/cholesky | solution.py:8
  278.8 0.6 compare_reduce_fusion
  279.5 0.7 fusion.19
  280.1 9.8 %custom-call.7 = f32[1,128,128]{1,2,0:T(8,128)S(1)} custom-call(f32[1,128,128]{2,1,0:T(8,128)S(1)} %get-tuple-element.15), custom_call_target="InvertDiagBlocksLowerTriangular" | custom-call | tf_op jit(solution)/shard_map/jit(_solve_triangular)/triangular_solve | solution.py:64
  289.9 0.7 copy.29
  290.7 1.9 fusion.14
  (15 shorter events, 0.2 us)
Async XLA Ops:
  33.2 7.8 %copy-start.1 = (s32[8,8]{1,0:T(8,128)S(1)}, s32[8,8]{1,0:T(8,128)}, u32[]{:S(2)}) copy-start(s32[8,8]{1,0:T(8,128)} %param.5) | copy-start | bytes 772
  33.3 8.4 %copy-start = (bf16[2048,128]{1,0:T(8,128)(2,1)S(1)}, bf16[2048,128]{1,0:T(8,128)(2,1)}, u32[]{:S(2)}) copy-start(bf16[2048,128]{1,0:T(8,128)(2,1)} %param.4) | copy-start | bytes 1572868
  33.3 121.0 %all-to-all-start = ((bf16[16,5,256,128]{3,2,1,0:T(8,128)(2,1)}), bf16[16,5,256,128]{3,2,1,0:T(8,128)(2,1)}, u32[]{:S(2)}, u32[]{:S(2)}) async-start(bf16[16,5,256,128]{3,2,1,0:T(8,128)(2,1)} %copy.22), calls=%async_computation | async-start | bytes 10485760 | tf_op jit(solution)/shard_map/all_to_all | solution.py:46
  41.0 224.3 %all-reduce.2.cloned.1.call-start = ((), (), s32[]{:S(2)}) async-start(), calls=%async_computation.1 | async-start | bytes 131072 | tf_op jit(solution)/shard_map/psum | solution.py:62
Sparse Core Ops, SparseCore 0:
  176.8 88.4 all-reduce.1
where the time goes:
time: 300 us; the launch traced here: 299 us
  waiting for transfers between devices  191 us (64%)
  local copies, waits for them, and re-layouts  26.6 us (9%)
  other arithmetic  25.3 us (8%)
  blocking collectives  19.3 us (6%)
  matrix products  15 us (5%)
  between operations  14.2 us (5%)
  starting transfers between devices  7.75 us (3%)
    all_to_all x1, waiting for transfers between devices, shards(): lax.all_to_all(outgoing, 'rows', split_axis=0, concat_axis=0, tiled=True)  103 us
    psum x1, waiting for transfers between devices, shards(): gram = lax.psum(gram_local, 'rows')  88.3 us
    all_gather x1, blocking collectives, shards(): lax.all_gather(pattern, 'rows', axis=0, tiled=True)  19.3 us
    another operation x3, other arithmetic, upper_factor_of(): return jnp.linalg.cholesky(matrix).T  12.4 us
    gather x2, local copies, waits for them, and re-layouts, shards(): jnp.take(incoming.reshape(rank_count * slot_depth, block_size, columns),...  12 us
    another operation x1, other arithmetic, shards(): jax.scipy.linalg.solve_triangular(factor.T, image.T, lower=True)  9.81 us
    gather x2, local copies, waits for them, and re-layouts, shards(): local_part = jnp.take(own_blocks, my_local, axis=0)  9.43 us
    dot_general x1, matrix products, shards(): jnp.einsum('rsij,rsjk->rik', a_blocks, operand, preferred_element_type=jn...  8.75 us
  transfers between devices with their start and end apart: 2, of which 2 were waited for; matrix products, arithmetic and copies ran while one was open for 3% of the time, Pallas kernels for 0%

commit v1 on v0

--- a/solution.py
+++ b/solution.py
@@ -59,7 +59,7 @@
     image = product.reshape(block_rows * block_size, columns)
     node_count = rank_count * block_rows * block_size
     gram_local = jnp.einsum("nk,nl->kl", image, image, precision=lax.Precision.HIGHEST)
-    gram = lax.psum(gram_local, "rows")
+    gram = jnp.sum(lax.all_gather(gram_local, "rows"), axis=0)
     factor = upper_factor_of(gram / node_count)
     basis_out = jax.scipy.linalg.solve_triangular(factor.T, image.T, lower=True).T
     return (basis_out, factor)

time: 300 us -> 252 us (0.84)
  waiting for transfers between devices: 191 us -> 141 us
    psum x1 -> x0, waiting for transfers between devices: 88.3 us -> none  [shards(): gram = lax.psum(gram_local, 'rows')]
    all_gather x0 -> x1, waiting for transfers between devices: none -> 38.2 us  [shards(): gram = jnp.sum(lax.all_gather(gram_local, 'rows'), axis=0)]
  transfers between devices with their start and end apart: 2 -> 2, of which waited for: 2 -> 2; matrix products, arithmetic and copies ran while one was open for 3% -> 4% of each run, Pallas kernels for 0% -> 0%
where the time goes in v1:
time: 252 us; the launch traced here: 249 us
  waiting for transfers between devices  141 us (56%)
  local copies, waits for them, and re-layouts  26.6 us (11%)
  other arithmetic  24.9 us (10%)
  blocking collectives  19.3 us (8%)
  matrix products  15 us (6%)
  between operations  14.2 us (6%)
  starting transfers between devices  7.75 us (3%)
    all_to_all x1, waiting for transfers between devices, shards(): lax.all_to_all(outgoing, 'rows', split_axis=0, concat_axis=0, tiled=True)  103 us
    all_gather x1, waiting for transfers between devices, shards(): gram = jnp.sum(lax.all_gather(gram_local, 'rows'), axis=0)  38.2 us
    all_gather x1, blocking collectives, shards(): lax.all_gather(pattern, 'rows', axis=0, tiled=True)  19.3 us
    another operation x3, other arithmetic, upper_factor_of(): return jnp.linalg.cholesky(matrix).T  12.4 us
    gather x2, local copies, waits for them, and re-layouts, shards(): jnp.take(incoming.reshape(rank_count * slot_depth, block_size, columns),...  12 us
    another operation x1, other arithmetic, shards(): jax.scipy.linalg.solve_triangular(factor.T, image.T, lower=True)  9.81 us
    gather x2, local copies, waits for them, and re-layouts, shards(): local_part = jnp.take(own_blocks, my_local, axis=0)  9.43 us
    dot_general x1, matrix products, shards(): jnp.einsum('rsij,rsjk->rik', a_blocks, operand, preferred_element_type=jn...  8.75 us
  transfers between devices with their start and end apart: 2, of which 2 were waited for; matrix products, arithmetic and copies ran while one was open for 4% of the time, Pallas kernels for 0%

profile of v1, /device:TPU:8, one launch (start us, length us, event | category | flops | bytes accessed | tf_op | source)
XLA Modules:
  0.0 249.0 jit_solution(11759628268833056247)
XLA Ops:
  7.2 19.3 %all_gather.9 = s32[128,8]{1,0:T(8,128)S(1)} all-gather(s32[8,8]{1,0:T(8,128)} %param.5), channel_id=1, replica_groups=mesh['groups'=2,'rows'=16] {'rows'}, dimensions={0}, use_global_device_ids=true | all-gather | bytes 4352 | tf_op jit(solution)/shard_map/all_gather | solution.py:22
  26.4 0.1 reshape.362
  26.5 0.1 fusion.33
  26.6 0.2 reduce_window_sum.23
  26.8 0.1 fusion.11
  27.0 2.5 %convolution_convert_fusion = bf16[16,5,256,128]{3,0,2,1:T(8,128)(2,1)S(1)} fusion(bf16[8,256,128]{2,1,0:T(8,128)(2,1)} %bitcast.43, bf16[16,5,8,1]{2,1,0,3:T(8,128)(2,1)S(1)} %fusion.11), kind=kOutput, calls=%fused_computation.9 | convolution fusion | flops 44564480 | bytes 5768448 | tf_op jit(solution)/shard_map/ekb,bij->ekij/dot_general | solution.py:43
  29.5 3.7 %copy.20 = bf16[16,5,256,128]{3,2,1,0:T(8,128)(2,1)} copy(bf16[16,5,256,128]{3,0,2,1:T(8,128)(2,1)S(1)} %convolution_convert_fusion) | data formatting | bytes 10485760 | tf_op jit(solution)/shard_map/convert_element_type | solution.py:45
  33.3 7.7 %all-to-all-start = ((bf16[16,5,256,128]{3,2,1,0:T(8,128)(2,1)}), bf16[16,5,256,128]{3,2,1,0:T(8,128)(2,1)}, u32[]{:S(2)}, u32[]{:S(2)}) async-start(bf16[16,5,256,128]{3,2,1,0:T(8,128)(2,1)} %copy.20), calls=%async_computation | async-start | bytes 10485760 | tf_op jit(solution)/shard_map/all_to_all | solution.py:46
  41.0 0.0 all-gather.3.cloned.1.call-start
  41.0 0.1 reshape.361
  41.1 0.1 reshape.365
  41.2 0.1 fusion.23
  41.3 0.1 reduce_window_sum.22
  41.4 0.2 select_reduce_fusion.1
  41.6 0.1 reduce_sum.25
  41.7 3.1 %gather_fusion.1 = bf16[64,256,128]{2,1,0:T(8,128)(2,1)} fusion(bf16[8,256,128]{2,1,0:T(8,128)(2,1)S(1)} %bitcast.44, s32[1024]{0:T(1024)S(1)} %pad_clamp_fusion), kind=kCustom, calls=%fused_computation.1 | custom fusion | bytes 8388864 | tf_op jit(solution)/shard_map/jit(_take)/gather | solution.py:54
  44.8 6.4 %copy.22 = bf16[64,256,128]{1,2,0:T(8,128)(2,1)} copy(bf16[64,256,128]{2,1,0:T(8,128)(2,1)} %gather_fusion.1) | data formatting | bytes 8388608 | tf_op jit(solution)/shard_map/jit(_take)/gather | solution.py:54
  51.2 103.1 %all-to-all-done = bf16[16,5,256,128]{3,2,1,0:T(8,128)(2,1)} async-done(((bf16[16,5,256,128]{3,2,1,0:T(8,128)(2,1)}), bf16[16,5,256,128]{3,2,1,0:T(8,128)(2,1)}, u32[]{:S(2)}, u32[]{:S(2)}) %all-to-all-start) | async-done | bytes 5242912 | tf_op jit(solution)/shard_map/all_to_all | solution.py:46
  154.3 5.6 %gather_fusion = bf16[64,256,128]{2,1,0:T(8,128)(2,1)} fusion(bf16[80,256,128]{2,1,0:T(8,128)(2,1)} %bitcast.3, s32[1024]{0:T(1024)S(1)} %pad_clamp_fusion.1), kind=kCustom, calls=%fused_computation | custom fusion | bytes 8388864 | tf_op jit(solution)/shard_map/jit(_take)/gather | solution.py:51
  159.8 6.4 %copy.21 = bf16[8,8,256,128]{2,3,1,0:T(8,128)(2,1)} copy(bf16[8,8,256,128]{3,2,1,0:T(8,128)(2,1)} %bitcast.45) | data formatting | bytes 8388608 | tf_op jit(solution)/shard_map/jit(_take)/gather | solution.py:51
  166.3 8.7 %fusion.8 = f32[8,256,128]{1,2,0:T(8,128)S(1)} fusion(bf16[8,8,256,256]{3,2,1,0:T(8,128)(2,1)} %param.3, bf16[8,8,256,128]{2,3,1,0:T(8,128)(2,1)} %bitcast.46, bf16[8,8,256,128]{2,3,1,0:T(8,128)(2,1)} %copy.21, pred[8,8]{1,0:T(8,128)(4,1)S(1)} %get-tuple-element.17, pred[8,8]{1,0:T(8,128)(4,1)S(1)} %get-tuple-element.18, pred[8,8]{1,0:T(8,128)(4,1)S(1)} %get-tuple-element.16), kind=kOutput, calls=%fused_computation.11 | convolution fusion | flops 1080033280 | bytes 17825984 | tf_op jit(solution)/shard_map/rsij,rsjk->rik/dot_general | solution.py:58
  175.0 1.6 convolution_bitcast_fusion
  176.7 0.3 copy.23
  177.0 38.2 %all-gather.3.cloned.1.call-done = f32[2048,128]{1,0:T(8,128)} async-done(((f32[128,128]{1,0:T(8,128)}), f32[2048,128]{1,0:T(8,128)}) %all-gather.3.cloned.1.call-update) | async-done | bytes 1048592 | tf_op jit(solution)/shard_map/all_gather | solution.py:62
  215.2 1.3 reduce_sum.27
  216.5 0.1 copy.25
  216.6 11.7 %cholesky.16 = f32[128,128]{1,0:T(8,128)S(1)} custom-call(f32[128,128]{1,0:T(8,128)S(1)} %fusion.16), custom_call_target="Cholesky" | custom-call | tf_op jit(solution)/shard_map/jit(cholesky)/cholesky | solution.py:8
  228.4 0.6 compare_reduce_fusion
  229.0 0.7 fusion.19
  229.7 9.8 %custom-call.7 = f32[1,128,128]{1,2,0:T(8,128)S(1)} custom-call(f32[1,128,128]{2,1,0:T(8,128)S(1)} %get-tuple-element.15), custom_call_target="InvertDiagBlocksLowerTriangular" | custom-call | tf_op jit(solution)/shard_map/jit(_solve_triangular)/triangular_solve | solution.py:64
  239.5 0.7 copy.26
  240.2 1.9 fusion.14
  (15 shorter events, 0.2 us)
Async XLA Ops:
  33.2 7.8 %copy-start.1 = (s32[8,8]{1,0:T(8,128)S(1)}, s32[8,8]{1,0:T(8,128)}, u32[]{:S(2)}) copy-start(s32[8,8]{1,0:T(8,128)} %param.5) | copy-start | bytes 772
  33.3 8.4 %copy-start = (bf16[2048,128]{1,0:T(8,128)(2,1)S(1)}, bf16[2048,128]{1,0:T(8,128)(2,1)}, u32[]{:S(2)}) copy-start(bf16[2048,128]{1,0:T(8,128)(2,1)} %param.4) | copy-start | bytes 1572868
  33.3 121.0 %all-to-all-start = ((bf16[16,5,256,128]{3,2,1,0:T(8,128)(2,1)}), bf16[16,5,256,128]{3,2,1,0:T(8,128)(2,1)}, u32[]{:S(2)}, u32[]{:S(2)}) async-start(bf16[16,5,256,128]{3,2,1,0:T(8,128)(2,1)} %copy.20), calls=%async_computation | async-start | bytes 10485760 | tf_op jit(solution)/shard_map/all_to_all | solution.py:46
  41.0 174.3 %all-gather.3.cloned.1.call-start = ((), (), s32[]{:S(2)}) async-start(), calls=%async_computation.1 | async-start | bytes 1114112 | tf_op jit(solution)/shard_map/all_gather | solution.py:62
Sparse Core Ops, SparseCore 0:
  176.8 38.3 all-gather.2
